TPU v7x, 128 devices: a whole 4x4x4 slice. The times are simulated.
128 devices in a mesh: row: 8 (over x, core), col: 16 (over y, z).
Axes of the slice: x: 4, y: 4, z: 4, core: 2. Of those that a mesh axis runs over, the one named last changes fastest.
Arguments:
- amplitudes: float32 [256, 32768], P(('row', 'col')), may hold values from -6 to 6
- integrals: float32 [16384, 32768], P('row', 'col'), may hold values from -0.09375 to 0.09375
- ij_irrep: int32 [256], replicated, may hold values from 0 to 7
- ab_irrep: int32 [16384], P('row'), may hold values from 0 to 7
- cd_irrep: int32 [32768], P('col'), may hold values from 0 to 7
Outputs:
- ladder_out: float32 [256, 16384], P(('row', 'col'))
All inputs are finite; a program needn't handle non-finite values.
Results may differ from a plain program's by a relative error of at most 0.000078.
Values sent between devices are 32-bit elements; how exact they have to be, the bound alone decides.
A program may use at most 64 MiB of HBM per device.

v0:
```python
import jax
import jax.numpy as jnp
from jax import lax
from jax.sharding import PartitionSpec as P


def contract(amp_block, integrals):
    return lax.dot_general(
        amp_block,
        integrals,
        (((1,), (1,)), ((), ())),
        precision=lax.Precision.HIGHEST,
        preferred_element_type=jnp.float32,
    )


def body(amplitudes, integrals, ij_irrep, ab_irrep, cd_irrep):
    by_column = lax.all_to_all(amplitudes, "col", split_axis=1, concat_axis=0, tiled=True)
    gathered = lax.all_gather(by_column, "row", axis=0, tiled=True)
    row_count = lax.axis_size("row")
    col_count = lax.axis_size("col")
    pair_count = gathered.shape[0]
    col_width = gathered.shape[1]
    own_pairs = pair_count // (row_count * col_count)
    ordered = (
        gathered.reshape(row_count, col_count, own_pairs, col_width)
        .transpose(1, 0, 2, 3)
        .reshape(pair_count, col_width)
    )
    pair_irrep = (
        ij_irrep.reshape(row_count, col_count, own_pairs).transpose(1, 0, 2).reshape(pair_count)
    )
    masked = jnp.where(cd_irrep[None, :] == pair_irrep[:, None], ordered, 0.0)
    product = contract(masked, integrals)
    shared = lax.psum_scatter(
        jnp.where(pair_irrep[:, None] == ab_irrep[None, :], product, 0.0),
        "col",
        scatter_dimension=0,
        tiled=True,
    )
    owned = lax.all_to_all(shared, "row", split_axis=0, concat_axis=1, tiled=True)
    return owned


def solution(mesh):
    in_specs = (P(("row", "col"), None), P("row", "col"), P(), P("row"), P("col"))
    out_specs = P(("row", "col"), None)
    return jax.shard_map(body, mesh=mesh, in_specs=in_specs, out_specs=out_specs, check_vma=False)
```

profile of v0, /device:TPU:1, one launch (start us, length us, event | category | flops | bytes accessed | tf_op | source)
XLA Modules:
  0.0 166.6 jit_solution(9258753089181089107)
XLA Ops:
  6.5 0.0 all-gather.2.cloned.1.call-start
  6.5 16.1 %all_to_all.38 = f32[2,16,2048]{2,0,1:T(2,128)S(1)} all-to-all(f32[2,16,2048]{2,0,1:T(2,128)} %bitcast.11), channel_id=1, replica_groups=mesh['row'=8,'col'=16] {'col'}, dimensions={1} | all-to-all | bytes 524288 | tf_op jit(solution)/shard_map/all_to_all | solution.py:18
  22.6 0.9 all_to_all.31
  23.5 0.0 all-gather.2.cloned.1.call-update
  23.5 0.0 reduce-scatter.2.cloned.1.call-start
  23.6 0.8 reshape.18
  24.4 0.1 eq.12
  24.5 24.0 %all-gather.2.cloned.1.call-done = f32[256,2048]{1,0:T(8,128)} async-done(((f32[32,2048]{1,0:T(8,128)}), f32[256,2048]{1,0:T(8,128)}) %all-gather.2.cloned.1.call-update) | async-done | bytes 2097168 | tf_op jit(solution)/shard_map/all_gather | solution.py:19
  48.5 2.5 %reshape.19 = f32[8,16,2,2048]{3,2,1,0:T(2,128)S(1)} reshape(f32[256,2048]{1,0:T(8,128)} %all-gather.2.cloned.1.call-done) | data formatting | bytes 4194304 | tf_op jit(solution)/shard_map/reshape | solution.py:26
  51.0 1.6 copy.9
  52.6 0.0 copy-start
  52.6 0.0 copy-start.1
  52.6 2.7 %reshape.20 = f32[256,2048]{1,0:T(8,128)S(1)} reshape(f32[16,8,2,2048]{3,2,1,0:T(2,128)} %copy.9) | data formatting | bytes 4194304 | tf_op jit(solution)/shard_map/reshape | solution.py:28
  55.3 0.0 copy-done
  55.3 0.0 copy-done.1
  55.3 18.1 %convolution_select_fusion = f32[256,2048]{1,0:T(8,128)} fusion(f32[2048,2048]{1,0:T(8,128)} %param.6, f32[256,2048]{1,0:T(8,128)S(1)} %reshape.20, s32[2048]{0:T(1024)S(1)} %copy-done, s32[2048]{0:T(1024)S(1)} %copy-done.1, s32[256]{0:T(256)S(1)} %eq.12), kind=kOutput, calls=%fused_computation | convolution fusion | flops 12886999040 | bytes 20988928 | tf_op jit(solution)/shard_map/dot_general | solution.py:8
  73.5 0.0 reduce-scatter.2.cloned.1.call-update
  73.5 73.0 %reduce-scatter.2.cloned.1.call-done = f32[16,2048]{1,0:T(8,128)} async-done(((f32[256,2048]{1,0:T(8,128)}), f32[16,2048]{1,0:T(8,128)}) %reduce-scatter.2.cloned.1.call-update) | async-done | bytes 131088 | tf_op jit(solution)/shard_map/reduce_scatter | solution.py:35
  146.5 1.0 all_to_all.32
  147.5 11.6 %all_to_all.39 = f32[8,2,2048]{2,1,0:T(2,128)S(1)} all-to-all(f32[8,2,2048]{2,1,0:T(2,128)S(1)} %all_to_all.32), channel_id=1, replica_groups=mesh['row'=8,'col'=16] {'row'}, dimensions={0} | all-to-all | bytes 262144 | tf_op jit(solution)/shard_map/all_to_all | solution.py:41
  159.1 0.7 copy.12
  (1 shorter events, 0.0 us)
Async XLA Ops:
  6.5 42.0 %all-gather.2.cloned.1.call-start = ((), (), s32[]{:S(2)}) async-start(), calls=%async_computation.3 | async-start | bytes 2359296 | tf_op jit(solution)/shard_map/all_gather | solution.py:19
  23.5 123.0 %reduce-scatter.2.cloned.1.call-start = ((), (), s32[]{:S(2)}) async-start(), calls=%async_computation.4 | async-start | bytes 2228224 | tf_op jit(solution)/shard_map/reduce_scatter | solution.py:35
  52.6 2.7 %copy-start = (s32[2048]{0:T(1024)S(1)}, s32[2048]{0:T(1024)}, u32[]{:S(2)}) copy-start(s32[2048]{0:T(1024)} %param.9) | copy-start | bytes 24580
  52.6 2.7 %copy-start.1 = (s32[2048]{0:T(1024)S(1)}, s32[2048]{0:T(1024)}, u32[]{:S(2)}) copy-start(s32[2048]{0:T(1024)} %param.8) | copy-start | bytes 24580
Sparse Core Ops, SparseCore 0:
  23.6 24.8 all-gather.1
  73.6 72.8 reduce-scatter.1
where the time goes:
time: 167 us
  waiting for transfers between devices  97 us (58%)
  blocking collectives  27.6 us (17%)
  matrix products  18.1 us (11%)
  between operations  13.5 us (8%)
  local copies, waits for them, and re-layouts  10.3 us (6%)
    reduce_scatter x1, waiting for transfers between devices, body(): lax.psum_scatter(jnp.where(pair_irrep[:, None] == ab_irrep[None, :], prod...  73 us
    all_gather x1, waiting for transfers between devices, body(): gathered = lax.all_gather(by_column, 'row', axis=0, tiled=True)  24 us
    dot_general x1, matrix products, contract(): lax.dot_general(amp_block, integrals, (((1,), (1,)), ((), ())), precision...  18.1 us
    all_to_all x1, blocking collectives, body(): lax.all_to_all(amplitudes, 'col', split_axis=1, concat_axis=0, tiled=True)  16.1 us
    all_to_all x1, blocking collectives, body(): lax.all_to_all(shared, 'row', split_axis=0, concat_axis=1, tiled=True)  11.6 us
  transfers between devices with their start and end apart: 2, of which 2 were waited for; matrix products, arithmetic and copies ran while one was open for 1% of the time, Pallas kernels for 0%

commit v1 on v0

v1 whole, which is shorter than its diff:
```python
import functools

import jax
import jax.numpy as jnp
from jax import lax
from jax.experimental import pallas as pl
from jax.experimental.pallas import tpu as pltpu
from jax.sharding import PartitionSpec as P

MESH = pl.DeviceIdType.MESH
ROWS, COLS = 8, 16
NIJ = 256
CAP = 64
BLOCK = 2048
SUB = BLOCK // ROWS
CHUNKS = 8
CHUNK = BLOCK // CHUNKS
SHARE = BLOCK // COLS
F32, BF16 = jnp.float32, jnp.bfloat16
NT = (((1,), (1,)), ((), ()))


def dot(a, b, dims=(((1,), (0,)), ((), ()))):
    return lax.dot_general(a, b, dims, preferred_element_type=F32)


def halves(v):
    hi = v.astype(BF16)
    return hi, (v - hi.astype(F32)).astype(BF16)


def column(row):
    return jnp.transpose(jnp.broadcast_to(row, (128, 128)))


def remote(src, dst, send, recv, row, col):
    return pltpu.make_async_remote_copy(
        src_ref=src, dst_ref=dst, send_sem=send, recv_sem=recv, device_id=(row, col), device_id_type=MESH
    )


def kernel(
    amp_ref, int_ref, ij_ref, ab_ref, cd_ref, out_ref,
    ints, parts, ab_col, hop, mine, packed, gathered, weights, sums, got, fin, swapped,
    int_sem, local_sem, send, recv,
):
    r, c = lax.axis_index("row"), lax.axis_index("col")
    x, core = r // 2, r % 2
    sibling = x * 2 + 1 - core

    barrier = pltpu.get_barrier_semaphore()
    for t in range(1, ROWS):
        pl.semaphore_signal(barrier, inc=1, device_id=((r + t) % ROWS, c), device_id_type=MESH)
    for t in range(1, COLS):
        pl.semaphore_signal(barrier, inc=1, device_id=(r, (c + t) % COLS), device_id_type=MESH)

    def fetch(q):
        rows = pl.ds(q * CHUNK, CHUNK)
        return pltpu.make_async_copy(int_ref.at[rows], ints.at[rows], int_sem.at[q])

    for q in range(CHUNKS):
        fetch(q).start()

    ij_row = jnp.broadcast_to(ij_ref[...], (8, NIJ)).astype(F32).astype(BF16)
    source = lax.broadcasted_iota(jnp.int32, (NIJ, NIJ), 0)
    target = lax.broadcasted_iota(jnp.int32, (NIJ, NIJ), 1)
    wanted = jnp.where(target < 128, 2 * target, 2 * target - 255)
    reorder = jnp.where(source == wanted, 1.0, 0.0).astype(F32).astype(BF16)
    key_row = dot(ij_row, reorder)[0:1, :]
    key_col = [column(key_row[:, 0:128]), column(key_row[:, 128:256])]
    keys = jnp.concatenate(key_col, axis=0)
    keys = jnp.concatenate([keys, keys], axis=1)
    same = keys == key_row
    rank_row = jnp.sum(jnp.where(same & (source < target), 1.0, 0.0), axis=0, keepdims=True)
    rank_col = jnp.sum(jnp.where(same & (target < source), 1.0, 0.0), axis=1, keepdims=True)

    for q in range(COLS):
        ab_col[pl.ds(q * 128, 128), :] = column(ab_ref[:, pl.ds(q * 128, 128)])

    def prepare(first, last):
        for q in range(first, last):
            fetch(q).wait()

            def step(s, carry, q=q):
                rows = pl.ds(pl.multiple_of(q * CHUNK + s * 16, 16), 16)
                label = ab_col[rows, :]
                for j in range(BLOCK // 128):
                    lanes = pl.ds(j * 128, 128)
                    value = jnp.where(label == cd_ref[:, lanes], ints[rows, lanes], 0.0)
                    hi, lo = halves(value)
                    at = pl.ds(pl.multiple_of(s * 16, 16), 16)
                    parts[q, at, lanes] = hi
                    parts[q, pl.ds(pl.multiple_of(CHUNK + s * 16, 16), 16), lanes] = lo
                return carry

            lax.fori_loop(0, CHUNK // 16, step, 0)

    prepare(0, 3)
    pl.semaphore_wait(barrier, ROWS + COLS - 2)

    for t in range(1, ROWS):
        to = (r + t) % ROWS
        remote(amp_ref.at[:, to], hop.at[r], send.at[0], recv.at[0], to, c).start()
    own = pltpu.make_async_copy(amp_ref.at[:, r], hop.at[r], local_sem.at[0])
    own.start()
    prepare(3, 5)
    own.wait()
    drain = remote(hop.at[pl.ds(0, ROWS - 1)], hop.at[pl.ds(0, ROWS - 1)], send.at[0], recv.at[0], r, c)
    drain.wait_recv()
    for t in range(1, COLS):
        to = (c + t) % COLS
        remote(hop.at[:, to], mine.at[:, c], send.at[1], recv.at[1], r, to).start()
    own = pltpu.make_async_copy(hop.at[:, c], mine.at[:, c], local_sem.at[1])
    own.start()
    drain.wait_send()
    prepare(5, 7)
    own.wait()
    some = mine.at[:, pl.ds(0, COLS - 1)]
    drain = remote(some, some, send.at[1], recv.at[1], r, c)
    drain.wait_recv()

    slot = lax.broadcasted_iota(jnp.int32, (CAP, 128), 0).astype(F32)
    for t in range(2):
        cd_row = cd_ref[:, pl.ds(pl.multiple_of(r * SUB + t * 128, 128), 128)].astype(F32)
        total = jnp.zeros((CAP, 128), F32)
        for i in range(2):
            amps = mine[:, :, t * 2 + i, :].reshape(128, 128)
            amps = jnp.where(key_col[i] == cd_row, amps, 0.0)
            pick = jnp.where(rank_row[:, i * 128 : (i + 1) * 128] == slot, 1.0, 0.0).astype(BF16)
            hi, lo = halves(amps)
            total += dot(pick, hi) + dot(pick, lo)
        packed[:, t * 128 : (t + 1) * 128] = total
    drain.wait_send()

    remote(packed, gathered.at[r], send.at[2], recv.at[2], sibling, c).start()
    for t in (1, 3, 2):
        remote(packed, gathered.at[r], send.at[3], recv.at[3 + t], (x + t) % 4 * 2 + core, c).start()
    own = pltpu.make_async_copy(packed, gathered.at[r], local_sem.at[2])
    own.start()
    prepare(7, 8)
    own.wait()
    for t in (1, 3, 2):
        k = (x + 4 - t) % 4 * 2 + core
        remote(gathered.at[k], gathered.at[k], send.at[3], recv.at[3 + t], r, c).wait_recv()
        remote(gathered.at[k], gathered.at[k], send.at[7], recv.at[2], sibling, c).start()
    four = gathered.at[pl.ds(0, 4)]
    three = gathered.at[pl.ds(0, 3)]
    remote(four, four, send.at[2], recv.at[2], r, c).wait_recv()
    for k in range(ROWS):
        hi, lo = halves(gathered[k])
        weights[0:CAP, k * SUB : (k + 1) * SUB] = hi
        weights[CAP : 2 * CAP, k * SUB : (k + 1) * SUB] = lo

    lane = lax.broadcasted_iota(jnp.int32, (SHARE // 2, 128), 1)

    def chunk(j, carry):
        q = (c // 2 + 1 + j) % CHUNKS
        both = dot(parts[q], weights[...], NT)
        both = both[0:CHUNK] + both[CHUNK:]
        both = both + pltpu.roll(both, CAP, 1)
        for s in range(CHUNK // SHARE):
            to = q * 2 + s
            low = both[s * SHARE : s * SHARE + SHARE // 2]
            high = both[s * SHARE + SHARE // 2 : (s + 1) * SHARE]
            sums[to] = jnp.where(lane < CAP, low, high)

            @pl.when(to != c)
            def _():
                remote(sums.at[to], got.at[c], send.at[8], recv.at[8], r, to).start()

        return carry

    lax.fori_loop(0, CHUNKS, chunk, 0)
    own = pltpu.make_async_copy(sums.at[c], got.at[c], local_sem.at[3])
    own.start()
    own.wait()
    some = got.at[pl.ds(0, COLS - 1)]
    drain = remote(some, some, send.at[8], recv.at[8], r, c)
    drain.wait_recv()
    total = got[0]
    for k in range(1, COLS):
        total += got[k]

    ab_row = ab_ref[:, pl.ds(pl.multiple_of(c * SHARE, 128), SHARE)].astype(F32)
    hi, lo = halves(total)
    place = lax.broadcasted_iota(jnp.int32, (128, 128), 1).astype(F32)
    for i in range(2):
        rank = rank_col[i * 128 : (i + 1) * 128]
        pieces = []
        for h in range(2):
            pick = jnp.where(rank + float(h * CAP) == place, 1.0, 0.0).astype(BF16)
            pieces.append(dot(pick, hi, NT) + dot(pick, lo, NT))
        rows = jnp.concatenate(pieces, axis=1)
        fin[:, :, i, :] = jnp.where(key_col[i] == ab_row, rows, 0.0).reshape(ROWS, COLS, 128)
    drain.wait_send()

    for t in range(1, COLS):
        to = (c + t) % COLS
        remote(fin.at[:, to], swapped.at[:, c], send.at[9], recv.at[9], r, to).start()
    own = pltpu.make_async_copy(fin.at[:, c], swapped.at[:, c], local_sem.at[4])
    own.start()
    own.wait()
    some = swapped.at[:, pl.ds(0, COLS - 1)]
    drain = remote(some, some, send.at[9], recv.at[9], r, c)
    drain.wait_recv()
    for t in range(1, ROWS):
        to = (r + t) % ROWS
        remote(swapped.at[to], out_ref.at[r], send.at[10], recv.at[10], to, c).start()
    own = pltpu.make_async_copy(swapped.at[r], out_ref.at[r], local_sem.at[5])
    own.start()
    own.wait()
    drain.wait_send()
    some = out_ref.at[pl.ds(0, ROWS - 1)]
    drain = remote(some, some, send.at[10], recv.at[10], r, c)
    drain.wait_recv()
    drain.wait_send()
    remote(packed, packed, send.at[2], recv.at[2], r, c).wait_send()
    remote(three, three, send.at[3], recv.at[2], r, c).wait_send()
    remote(three, three, send.at[7], recv.at[2], r, c).wait_send()


def packed_body(amplitudes, integrals, ij_irrep, ab_irrep, cd_irrep):
    amps = amplitudes.reshape(2, COLS, ROWS, 2, 128).transpose(1, 2, 3, 0, 4).reshape(COLS, ROWS, 4, 128)
    vmem = pl.BlockSpec(memory_space=pltpu.VMEM)
    hbm = pl.BlockSpec(memory_space=pl.ANY)
    out = pl.pallas_call(
        kernel,
        out_shape=jax.ShapeDtypeStruct((ROWS, COLS, 2, 128), F32),
        in_specs=[hbm, hbm, vmem, vmem, vmem],
        out_specs=vmem,
        scratch_shapes=[
            pltpu.VMEM((BLOCK, BLOCK), F32),
            pltpu.VMEM((CHUNKS, 2 * CHUNK, BLOCK), BF16),
            pltpu.VMEM((BLOCK, 128), jnp.int32),
            pltpu.VMEM((ROWS, COLS, 4, 128), F32),
            pltpu.VMEM((ROWS, COLS, 4, 128), F32),
            pltpu.VMEM((CAP, SUB), F32),
            pltpu.VMEM((ROWS, CAP, SUB), F32),
            pltpu.VMEM((2 * CAP, BLOCK), BF16),
            pltpu.VMEM((COLS, SHARE // 2, 128), F32),
            pltpu.VMEM((COLS, SHARE // 2, 128), F32),
            pltpu.VMEM((ROWS, COLS, 2, 128), F32),
            pltpu.VMEM((ROWS, COLS, 2, 128), F32),
            pltpu.SemaphoreType.DMA((CHUNKS,)),
            pltpu.SemaphoreType.DMA((6,)),
            pltpu.SemaphoreType.DMA((11,)),
            pltpu.SemaphoreType.DMA((11,)),
        ],
        compiler_params=pltpu.CompilerParams(collective_id=0, has_side_effects=True, vmem_limit_bytes=58 << 20),
        name="packed_ladder",
    )(amps, integrals, ij_irrep.reshape(1, -1), ab_irrep.reshape(1, -1), cd_irrep.reshape(1, -1))
    return out.reshape(ROWS * COLS, 2, 128).transpose(1, 0, 2).reshape(2, ROWS * COLS * 128)


def plain_body(amplitudes, integrals, ij_irrep, ab_irrep, cd_irrep):
    by_column = lax.all_to_all(amplitudes, "col", split_axis=1, concat_axis=0, tiled=True)
    gathered = lax.all_gather(by_column, "row", axis=0, tiled=True)
    own_pairs = NIJ // (ROWS * COLS)
    ordered = gathered.reshape(ROWS, COLS, own_pairs, BLOCK).transpose(1, 0, 2, 3).reshape(NIJ, BLOCK)
    pair_irrep = ij_irrep.reshape(ROWS, COLS, own_pairs).transpose(1, 0, 2).reshape(NIJ)
    masked = jnp.where(cd_irrep[None, :] == pair_irrep[:, None], ordered, 0.0)
    product = lax.dot_general(
        masked, integrals, NT, precision=lax.Precision.HIGHEST, preferred_element_type=F32
    )
    product = jnp.where(pair_irrep[:, None] == ab_irrep[None, :], product, 0.0)
    shared = lax.psum_scatter(product, "col", scatter_dimension=0, tiled=True)
    return lax.all_to_all(shared, "row", split_axis=0, concat_axis=1, tiled=True)


def body(amplitudes, integrals, ij_irrep, ab_irrep, cd_irrep):
    sizes = jnp.sum(ij_irrep[None, :] == jnp.arange(8, dtype=jnp.int32)[:, None], axis=1)
    fits = jnp.max(sizes) <= CAP
    return lax.cond(fits, packed_body, plain_body, amplitudes, integrals, ij_irrep, ab_irrep, cd_irrep)


def solution(mesh):
    in_specs = (P(("row", "col"), None), P("row", "col"), P(), P("row"), P("col"))
    out_specs = P(("row", "col"), None)
    return jax.shard_map(body, mesh=mesh, in_specs=in_specs, out_specs=out_specs, check_vma=False)
```

time: 167 us -> 65.7 us (0.39)
  waiting for transfers between devices: 97 us -> 0 us
  Pallas kernels: 0 us -> 49.4 us
  blocking collectives: 27.6 us -> 0 us
  matrix products: 18.1 us -> 0 us
  local copies, waits for them, and re-layouts: 10.3 us -> 0.66 us
    reduce_scatter x1 -> x0, waiting for transfers between devices: 73 us -> none  [body(): lax.psum_scatter(jnp.where(pair_irrep[:, None] == ab_irrep[None, :], prod...]
    pallas_call x0 -> x1, Pallas kernels: none -> 49.4 us  [packed_body(): pl.pallas_call(kernel, out_shape=jax.ShapeDtypeStruct((ROWS, COLS, 2, 128...]
    all_to_all x2 -> x0, blocking collectives: 27.6 us -> none  [the longest x1 16.1 us: body(): lax.all_to_all(amplitudes, 'col', split_axis=1, concat_axis=0, tiled=True)]
    all_gather x1 -> x0, waiting for transfers between devices: 24 us -> none  [body(): gathered = lax.all_gather(by_column, 'row', axis=0, tiled=True)]
    dot_general x1 -> x0, matrix products: 18.1 us -> none  [contract(): lax.dot_general(amp_block, integrals, (((1,), (1,)), ((), ())), precision...]
    reshape x3 -> x0, local copies, waits for them, and re-layouts: 6.02 us -> none  [the longest x1 2.72 us: body(): ordered = gathered.reshape(row_count, col_count, own_pairs, col_width).tr...]
    all_to_all x2 -> x0, local copies, waits for them, and re-layouts: 1.87 us -> none  [the longest x1 0.98 us: body(): lax.all_to_all(shared, 'row', split_axis=0, concat_axis=1, tiled=True)]
  transfers between devices with their start and end apart: 2 -> 0, of which waited for: 2 -> 0; matrix products, arithmetic and copies ran while one was open for 1% -> 0% of each run, Pallas kernels for 0% -> 0%
where the time goes in v1:
time: 65.7 us; the launch traced here: 65.5 us
  Pallas kernels  49.4 us (75%)
  between operations  14 us (21%)
  other arithmetic  1.43 us (2%)
  local copies, waits for them, and re-layouts  0.66 us (1%)
    pallas_call x1, Pallas kernels, packed_body(): pl.pallas_call(kernel, out_shape=jax.ShapeDtypeStruct((ROWS, COLS, 2, 128...  49.4 us

profile of v1, /device:TPU:1, one launch (start us, length us, event | category | flops | bytes accessed | tf_op | source)
XLA Modules:
  0.0 65.5 jit_solution(10902288506650481092)
XLA Ops:
  6.5 0.8 %convert_reduce_fusion = s32[8]{0:T(128)S(1)} fusion(s32[256]{0:T(256)} %param.9), kind=kLoop, calls=%fused_computation.7 | loop fusion | flops 6136 | bytes 1056 | tf_op jit(solution)/shard_map/reduce_sum | solution.py:271
  7.3 0.6 reduce_max.9
  8.6 49.4 %conditional.1 = (f32[2,16384]{1,0:T(2,128)S(1)}) conditional(s32[]{:T(128)} %convert_element_type.7, (s32[256]{0:T(256)}, s32[2048]{0:T(1024)}, s32[2048]{0:T(1024)}, f32[2,32768]{1,0:T(2,128)}, f32[2048,2048]{1,0:T(8,128)}) %tuple.11, (f32[2,32768]{1,0:T(2,128)}, s32[256]{0:T(256)}, s32[2048]{0:T(1024)}, s32[2048]{0:T(1024)}, ...), branch_computations={%region_2.4_spmd, %region_4.5_spmd} | conditional | flops 12886999040 | bytes 48979088 | solution.py:273
  8.6 49.4 %packed_ladder.1 = f32[8,16,2,128]{3,2,1,0:T(2,128)S(1)} custom-call(f32[16,8,4,128]{3,2,1,0:T(4,128)} %bitcast.23, f32[2048,2048]{1,0:T(8,128)} %get-tuple-element.34.int_ref, s32[1,256]{1,0:T(1,128)} %bitcast.30, s32[1,2048]{1,0:T(1,128)} %bitcast.29, s32[1,2048]{1,0:T(1,128)} %bitcast.28), custom_call_target="tpu_custom_call" | custom-call | tf_op jit(solution)/shard_map/cond/branch_1_fun/packed_ladder/pallas_call | solution.py:226
  58.0 0.7 %copy.20 = f32[2,16384]{1,0:T(2,128)} copy(f32[2,16384]{1,0:T(2,128)S(1)} %get-tuple-element.38) | data formatting | bytes 262144

commit v2 on v1

--- a/solution.py
+++ b/solution.py
@@ -40,8 +40,8 @@
 
 
 def kernel(
-    amp_ref, int_ref, ij_ref, ab_ref, cd_ref, out_ref,
-    ints, parts, ab_col, hop, mine, packed, gathered, weights, sums, got, fin, swapped,
+    base_ref, amp_ref, int_ref, ij_ref, ab_ref, cd_ref, out_ref, most_ref,
+    ints, parts, ab_col, hop, mine, packed, gathered, sums, shares, got, fin, swapped,
     int_sem, local_sem, send, recv,
 ):
     r, c = lax.axis_index("row"), lax.axis_index("col")
@@ -73,6 +73,11 @@
     same = keys == key_row
     rank_row = jnp.sum(jnp.where(same & (source < target), 1.0, 0.0), axis=0, keepdims=True)
     rank_col = jnp.sum(jnp.where(same & (target < source), 1.0, 0.0), axis=1, keepdims=True)
+    most_ref[...] = jnp.broadcast_to(jnp.max(rank_row, axis=1, keepdims=True) + 1.0, (8, 128)).astype(jnp.int32)
+    base = base_ref[...].astype(F32)
+    rank_row = rank_row - base[0:1, 0:1]
+    rank_col = rank_col - base[0:1, 0:1]
+    rank_col = jnp.where((rank_col >= 0.0) & (rank_col < float(CAP)), rank_col, -1.0 - 2 * CAP)
 
     for q in range(COLS):
         ab_col[pl.ds(q * 128, 128), :] = column(ab_ref[:, pl.ds(q * 128, 128)])
@@ -95,7 +100,7 @@
 
             lax.fori_loop(0, CHUNK // 16, step, 0)
 
-    prepare(0, 3)
+    prepare(0, 2)
     pl.semaphore_wait(barrier, ROWS + COLS - 2)
 
     for t in range(1, ROWS):
@@ -103,7 +108,7 @@
         remote(amp_ref.at[:, to], hop.at[r], send.at[0], recv.at[0], to, c).start()
     own = pltpu.make_async_copy(amp_ref.at[:, r], hop.at[r], local_sem.at[0])
     own.start()
-    prepare(3, 5)
+    prepare(2, 5)
     own.wait()
     drain = remote(hop.at[pl.ds(0, ROWS - 1)], hop.at[pl.ds(0, ROWS - 1)], send.at[0], recv.at[0], r, c)
     drain.wait_recv()
@@ -113,7 +118,7 @@
     own = pltpu.make_async_copy(hop.at[:, c], mine.at[:, c], local_sem.at[1])
     own.start()
     drain.wait_send()
-    prepare(5, 7)
+    prepare(5, 8)
     own.wait()
     some = mine.at[:, pl.ds(0, COLS - 1)]
     drain = remote(some, some, send.at[1], recv.at[1], r, c)
@@ -135,43 +140,60 @@
     remote(packed, gathered.at[r], send.at[2], recv.at[2], sibling, c).start()
     for t in (1, 3, 2):
         remote(packed, gathered.at[r], send.at[3], recv.at[3 + t], (x + t) % 4 * 2 + core, c).start()
-    own = pltpu.make_async_copy(packed, gathered.at[r], local_sem.at[2])
-    own.start()
-    prepare(7, 8)
-    own.wait()
-    for t in (1, 3, 2):
+
+    def arrived(k, sem):
+        remote(gathered.at[k], gathered.at[k], send.at[3], recv.at[sem], r, c).wait_recv()
+
+    def forward(t):
         k = (x + 4 - t) % 4 * 2 + core
-        remote(gathered.at[k], gathered.at[k], send.at[3], recv.at[3 + t], r, c).wait_recv()
-        remote(gathered.at[k], gathered.at[k], send.at[7], recv.at[2], sibling, c).start()
-    four = gathered.at[pl.ds(0, 4)]
-    three = gathered.at[pl.ds(0, 3)]
-    remote(four, four, send.at[2], recv.at[2], r, c).wait_recv()
-    for k in range(ROWS):
-        hi, lo = halves(gathered[k])
-        weights[0:CAP, k * SUB : (k + 1) * SUB] = hi
-        weights[CAP : 2 * CAP, k * SUB : (k + 1) * SUB] = lo
+        arrived(k, 3 + t)
+        remote(gathered.at[k], gathered.at[k], send.at[7], recv.at[10 + t], sibling, c).start()
+
+    def accumulate(t, finish=None):
+        chip = (x + 4 - t) % 4
+        if t:
+            arrived(chip * 2 + 1 - core, 10 + t)
+            values = [gathered[chip * 2], gathered[chip * 2 + 1]]
+        else:
+            arrived(sibling, 2)
+            own, other = packed[...], gathered[sibling]
+            values = [jnp.where(core == 0, own, other), jnp.where(core == 0, other, own)]
+        his, los = zip(*(halves(v) for v in values))
+        weights = jnp.concatenate([jnp.concatenate(his, axis=1), jnp.concatenate(los, axis=1)], axis=0)
+        lanes = pl.ds(pl.multiple_of(chip * 2 * SUB, 2 * SUB), 2 * SUB)
+        for dy, dz in ((2, 1), (2, 0), (1, 1), (3, 1), (1, 0), (3, 0), (0, 1), (0, 0)):
+            q = (c // 4 + dy) % 4 * 2 + (c % 4 // 2 + dz) % 2
+            both = dot(parts[q, :, lanes], weights, NT)
+            both = both[0:CHUNK] + both[CHUNK:]
+            if t:
+                both += sums[q]
+            if finish is None:
+                sums[q] = both
+            else:
+                finish(q, both)
 
     lane = lax.broadcasted_iota(jnp.int32, (SHARE // 2, 128), 1)
 
-    def chunk(j, carry):
-        q = (c // 2 + 1 + j) % CHUNKS
-        both = dot(parts[q], weights[...], NT)
-        both = both[0:CHUNK] + both[CHUNK:]
+    def finish(q, both):
         both = both + pltpu.roll(both, CAP, 1)
         for s in range(CHUNK // SHARE):
             to = q * 2 + s
             low = both[s * SHARE : s * SHARE + SHARE // 2]
             high = both[s * SHARE + SHARE // 2 : (s + 1) * SHARE]
-            sums[to] = jnp.where(lane < CAP, low, high)
+            shares[to] = jnp.where(lane < CAP, low, high)
 
             @pl.when(to != c)
             def _():
-                remote(sums.at[to], got.at[c], send.at[8], recv.at[8], r, to).start()
-
-        return carry
-
-    lax.fori_loop(0, CHUNKS, chunk, 0)
-    own = pltpu.make_async_copy(sums.at[c], got.at[c], local_sem.at[3])
+                remote(shares.at[to], got.at[c], send.at[8], recv.at[8], r, to).start()
+
+    accumulate(0)
+    forward(1)
+    forward(3)
+    accumulate(1)
+    forward(2)
+    accumulate(3)
+    accumulate(2, finish)
+    own = pltpu.make_async_copy(shares.at[c], got.at[c], local_sem.at[3])
     own.start()
     own.wait()
     some = got.at[pl.ds(0, COLS - 1)]
@@ -215,19 +237,22 @@
     drain.wait_recv()
     drain.wait_send()
     remote(packed, packed, send.at[2], recv.at[2], r, c).wait_send()
+    three = gathered.at[pl.ds(0, 3)]
     remote(three, three, send.at[3], recv.at[2], r, c).wait_send()
     remote(three, three, send.at[7], recv.at[2], r, c).wait_send()
 
 
-def packed_body(amplitudes, integrals, ij_irrep, ab_irrep, cd_irrep):
-    amps = amplitudes.reshape(2, COLS, ROWS, 2, 128).transpose(1, 2, 3, 0, 4).reshape(COLS, ROWS, 4, 128)
+def packed_round(base, amps, integrals, ij_irrep, ab_irrep, cd_irrep):
     vmem = pl.BlockSpec(memory_space=pltpu.VMEM)
     hbm = pl.BlockSpec(memory_space=pl.ANY)
-    out = pl.pallas_call(
+    out, most = pl.pallas_call(
         kernel,
-        out_shape=jax.ShapeDtypeStruct((ROWS, COLS, 2, 128), F32),
-        in_specs=[hbm, hbm, vmem, vmem, vmem],
-        out_specs=vmem,
+        out_shape=(
+            jax.ShapeDtypeStruct((ROWS, COLS, 2, 128), F32),
+            jax.ShapeDtypeStruct((8, 128), jnp.int32),
+        ),
+        in_specs=[vmem, hbm, hbm, vmem, vmem, vmem],
+        out_specs=(vmem, vmem),
         scratch_shapes=[
             pltpu.VMEM((BLOCK, BLOCK), F32),
             pltpu.VMEM((CHUNKS, 2 * CHUNK, BLOCK), BF16),
@@ -236,41 +261,36 @@
             pltpu.VMEM((ROWS, COLS, 4, 128), F32),
             pltpu.VMEM((CAP, SUB), F32),
             pltpu.VMEM((ROWS, CAP, SUB), F32),
-            pltpu.VMEM((2 * CAP, BLOCK), BF16),
+            pltpu.VMEM((CHUNKS, CHUNK, 128), F32),
             pltpu.VMEM((COLS, SHARE // 2, 128), F32),
             pltpu.VMEM((COLS, SHARE // 2, 128), F32),
             pltpu.VMEM((ROWS, COLS, 2, 128), F32),
             pltpu.VMEM((ROWS, COLS, 2, 128), F32),
             pltpu.SemaphoreType.DMA((CHUNKS,)),
             pltpu.SemaphoreType.DMA((6,)),
-            pltpu.SemaphoreType.DMA((11,)),
-            pltpu.SemaphoreType.DMA((11,)),
+            pltpu.SemaphoreType.DMA((14,)),
+            pltpu.SemaphoreType.DMA((14,)),
         ],
         compiler_params=pltpu.CompilerParams(collective_id=0, has_side_effects=True, vmem_limit_bytes=58 << 20),
-        name="packed_ladder",
-    )(amps, integrals, ij_irrep.reshape(1, -1), ab_irrep.reshape(1, -1), cd_irrep.reshape(1, -1))
-    return out.reshape(ROWS * COLS, 2, 128).transpose(1, 0, 2).reshape(2, ROWS * COLS * 128)
-
-
-def plain_body(amplitudes, integrals, ij_irrep, ab_irrep, cd_irrep):
-    by_column = lax.all_to_all(amplitudes, "col", split_axis=1, concat_axis=0, tiled=True)
-    gathered = lax.all_gather(by_column, "row", axis=0, tiled=True)
-    own_pairs = NIJ // (ROWS * COLS)
-    ordered = gathered.reshape(ROWS, COLS, own_pairs, BLOCK).transpose(1, 0, 2, 3).reshape(NIJ, BLOCK)
-    pair_irrep = ij_irrep.reshape(ROWS, COLS, own_pairs).transpose(1, 0, 2).reshape(NIJ)
-    masked = jnp.where(cd_irrep[None, :] == pair_irrep[:, None], ordered, 0.0)
-    product = lax.dot_general(
-        masked, integrals, NT, precision=lax.Precision.HIGHEST, preferred_element_type=F32
-    )
-    product = jnp.where(pair_irrep[:, None] == ab_irrep[None, :], product, 0.0)
-    shared = lax.psum_scatter(product, "col", scatter_dimension=0, tiled=True)
-    return lax.all_to_all(shared, "row", split_axis=0, concat_axis=1, tiled=True)
+        name="packed_round",
+    )(base, amps, integrals, ij_irrep, ab_irrep, cd_irrep)
+    return out.reshape(ROWS * COLS, 2, 128).transpose(1, 0, 2).reshape(2, ROWS * COLS * 128), most
 
 
 def body(amplitudes, integrals, ij_irrep, ab_irrep, cd_irrep):
-    sizes = jnp.sum(ij_irrep[None, :] == jnp.arange(8, dtype=jnp.int32)[:, None], axis=1)
-    fits = jnp.max(sizes) <= CAP
-    return lax.cond(fits, packed_body, plain_body, amplitudes, integrals, ij_irrep, ab_irrep, cd_irrep)
+    amps = amplitudes.reshape(2, COLS, ROWS, 2, 128).transpose(1, 2, 3, 0, 4).reshape(COLS, ROWS, 4, 128)
+    rest = (amps, integrals, ij_irrep.reshape(1, -1), ab_irrep.reshape(1, -1), cd_irrep.reshape(1, -1))
+    out, most = packed_round(jnp.zeros((1, 128), jnp.int32), *rest)
+
+    def more(state):
+        return state[0] < most[0, 0]
+
+    def another(state):
+        base, so_far = state
+        return base + CAP, so_far + packed_round(jnp.full((1, 128), base, jnp.int32), *rest)[0]
+
+    _, out = lax.while_loop(more, another, (jnp.int32(CAP), out))
+    return out
 
 
 def solution(mesh):

time: 65.7 us -> 52 us (0.79)
  between operations: 14 us -> 0.06 us
  local copies, waits for them, and re-layouts: 0.66 us -> 2.54 us
  other arithmetic: 1.43 us -> 0 us
  Pallas kernels: 49.4 us -> 48.3 us
  loops' own time: 0.02 us -> 0.88 us
    slice x0 -> x1, local copies, waits for them, and re-layouts: none -> 1.27 us  [more(): return state[0] < most[0, 0]]
    pallas_call x1, Pallas kernels: 49.4 us -> 48.3 us  [packed_round(): pl.pallas_call(kernel, out_shape=(jax.ShapeDtypeStruct((ROWS, COLS, 2, 12...]
    another operation x1, loops' own time: 0.02 us -> 0.88 us  [body(): _, out = lax.while_loop(more, another, (jnp.int32(CAP), out))]
    reduce_sum x1 -> x0, other arithmetic: 0.79 us -> none  [body(): jnp.sum(ij_irrep[None, :] == jnp.arange(8, dtype=jnp.int32)[:, None], axi...]
where the time goes in v2:
time: 52 us; the launch traced here: 51.8 us
  Pallas kernels  48.3 us (93%)
  local copies, waits for them, and re-layouts  2.54 us (5%)
  loops' own time  0.88 us (2%)
    pallas_call x1, Pallas kernels, packed_round(): pl.pallas_call(kernel, out_shape=(jax.ShapeDtypeStruct((ROWS, COLS, 2, 12...  48.3 us
    slice x1, local copies, waits for them, and re-layouts, more(): return state[0] < most[0, 0]  1.27 us

profile of v2, /device:TPU:1, one launch (start us, length us, event | category | flops | bytes accessed | tf_op | source)
XLA Modules:
  0.0 51.8 jit_solution(16016337668631476289)
XLA Ops:
  0.0 0.0 copy-start.2
  0.0 0.0 copy-start.1
  0.0 0.0 copy-start.3
  0.0 0.0 copy-start
  0.0 0.6 %broadcast_in_dim.6.base_ref = s32[1,128]{1,0:T(1,128)} broadcast(s32[]{:T(128)} %constant.2.clone.1), dimensions={} | broadcast | bytes 516 | tf_op jit(solution)/shard_map/broadcast_in_dim | solution.py:283
  0.6 48.3 %packed_round.2 = (f32[8,16,2,128]{3,2,1,0:T(2,128)S(1)}, s32[8,128]{1,0:T(8,128)}) custom-call(s32[1,128]{1,0:T(1,128)} %broadcast_in_dim.6.base_ref, f32[16,8,4,128]{3,2,1,0:T(4,128)} %bitcast.22, f32[2048,2048]{1,0:T(8,128)} %int_ref.1, s32[1,256]{1,0:T(1,128)} %bitcast.30, s32[1,2048]{1,0:T(1,128)} %bitcast.26, s32[1,2048]{1,0:T(1,128)} %bitcast.28), custom_call_target="tpu_custom_call" | custom-call | tf_op jit(solution)/shard_map/packed_round/pallas_call | solution.py:248
  49.0 0.0 copy-done.2
  49.0 0.0 copy-done.1
  49.0 0.0 copy-done.3
  49.0 0.0 copy-done
  49.0 2.2 %while.10 = (s32[]{:T(128)}, f32[2,16384]{1,0:T(2,128)S(1)}, s32[8,128]{1,0:T(8,128)}, f32[16,8,4,128]{3,2,1,0:T(4,128)S(1)}, f32[2048,2048]{1,0:T(8,128)}, /*in...) while((s32[]{:T(128)}, f32[2,16384]{1,0:T(2,128)S(1)}, ...), condition=%wide.region_1.0_spmd, body=%wide.region_0.0_spmd.sunk | while | flops 32770 | bytes 393841 | solution.py:292
  49.0 1.3 %slice.3 = s32[1,1]{1,0:T(1,128)} slice(s32[8,128]{1,0:T(8,128)} %get-tuple-element.79), slice={[0:1], [0:1]} | slice | bytes 8 | tf_op jit(solution)/shard_map/while/cond/slice | solution.py:286
  51.2 0.7 %copy.14 = f32[2,16384]{1,0:T(2,128)} copy(f32[2,16384]{1,0:T(2,128)S(1)} %get-tuple-element.53) | data formatting | bytes 262144
Async XLA Ops:
  0.0 49.0 %copy-start.2 = (s32[2048]{0:T(1024)S(1)}, s32[2048]{0:T(1024)}, u32[]{:S(2)}) copy-start(s32[2048]{0:T(1024)} %param.11) | copy-start | bytes 24580
  0.0 49.0 %copy-start.1 = (s32[2048]{0:T(1024)S(1)}, s32[2048]{0:T(1024)}, u32[]{:S(2)}) copy-start(s32[2048]{0:T(1024)} %param.10) | copy-start | bytes 24580
  0.0 49.0 %copy-start.3 = (s32[256]{0:T(256)S(1)}, s32[256]{0:T(256)}, u32[]{:S(2)}) copy-start(s32[256]{0:T(256)} %param.9) | copy-start | bytes 3076
  0.0 49.0 %copy-start = (f32[2,32768]{1,0:T(2,128)S(1)}, f32[2,32768]{1,0:T(2,128)}, u32[]{:S(2)}) copy-start(f32[2,32768]{1,0:T(2,128)} %param.7) | copy-start | bytes 786436

commit v3 on v2

v3 whole, which is shorter than its diff:
```python
import jax
import jax.numpy as jnp
import numpy as np
from jax import lax
from jax.experimental import pallas as pl
from jax.experimental.pallas import tpu as pltpu
from jax.sharding import PartitionSpec as P

MESH = pl.DeviceIdType.MESH
ROWS, COLS = 8, 16
XS = 4
NIJ = 256
HALF = NIJ // 2
CAP = 32
BLOCK = 2048
WIDE = BLOCK // XS
CHUNKS = 8
CHUNK = BLOCK // CHUNKS
SHARE = BLOCK // COLS
F32, BF16 = jnp.float32, jnp.bfloat16
NT = (((1,), (1,)), ((), ()))


def dot(a, b, dims=(((1,), (0,)), ((), ()))):
    return lax.dot_general(a, b, dims, preferred_element_type=F32)


def halves(v):
    hi = v.astype(BF16)
    return hi, (v - hi.astype(F32)).astype(BF16)


def column(row):
    return jnp.transpose(jnp.broadcast_to(row, (128, 128)))


def remote(src, dst, send, recv, row, col):
    return pltpu.make_async_remote_copy(
        src_ref=src, dst_ref=dst, send_sem=send, recv_sem=recv, device_id=(row, col), device_id_type=MESH
    )


def kernel(
    base_ref, amp_ref, int_ref, ij_ref, ab_ref, cd_ref, out_ref, most_ref,
    ints, parts, ab_col, mine, packed, gathered, sums, shares, got, fin,
    int_sem, local_sem, send, recv,
):
    r, c = lax.axis_index("row"), lax.axis_index("col")
    x, core = r // 2, r % 2
    sibling = x * 2 + 1 - core

    barrier = pltpu.get_barrier_semaphore()
    place_of = x * COLS + c
    pl.semaphore_signal(barrier, inc=1, device_id=(sibling, c), device_id_type=MESH)

    def greet(t, carry):
        peer = (place_of + t) % (XS * COLS)
        pl.semaphore_signal(barrier, inc=1, device_id=(peer // COLS * 2 + core, peer % COLS), device_id_type=MESH)
        return carry

    lax.fori_loop(1, XS * COLS, greet, 0)

    def fetch(q):
        rows = pl.ds(q * CHUNK, CHUNK)
        return pltpu.make_async_copy(int_ref.at[rows], ints.at[rows], int_sem.at[q])

    for q in range(CHUNKS):
        fetch(q).start()

    ij_row = jnp.broadcast_to(ij_ref[...], (8, NIJ)).astype(F32).astype(BF16)
    source = lax.broadcasted_iota(jnp.int32, (NIJ, NIJ), 0)
    target = lax.broadcasted_iota(jnp.int32, (NIJ, NIJ), 1)
    wanted = (target // 16 % 4) * 64 + (target // 128) * 32 + (target % 16) * 2 + (target // 64 % 2)
    reorder = jnp.where(source == wanted, 1.0, 0.0).astype(F32).astype(BF16)
    key_row = dot(ij_row, reorder)[0:1, :]
    key_col = [column(key_row[:, 0:HALF]), column(key_row[:, HALF:NIJ])]
    keys = jnp.concatenate(key_col, axis=0)
    keys = jnp.concatenate([keys, keys], axis=1)
    same = (keys == key_row) & (source // HALF == target // HALF)
    rank_row = jnp.sum(jnp.where(same & (source < target), 1.0, 0.0), axis=0, keepdims=True)
    rank_col = jnp.sum(jnp.where(same & (target < source), 1.0, 0.0), axis=1, keepdims=True)
    most_ref[...] = jnp.broadcast_to(jnp.max(rank_row, axis=1, keepdims=True) + 1.0, (8, 128)).astype(jnp.int32)
    base = base_ref[...].astype(F32)
    rank_row = rank_row - base[0:1, 0:1]
    rank_col = rank_col - base[0:1, 0:1]
    rank_col = jnp.where((rank_col >= 0.0) & (rank_col < float(CAP)), rank_col, -4.0 * NIJ)

    for q in range(COLS):
        ab_col[pl.ds(q * 128, 128), :] = column(ab_ref[:, pl.ds(q * 128, 128)])

    def prepare(first, last):
        for q in range(first, last):
            fetch(q).wait()

            def step(s, carry, q=q):
                rows = pl.ds(pl.multiple_of(q * CHUNK + s * 16, 16), 16)
                label = ab_col[rows, :]
                for j in range(BLOCK // 128):
                    lanes = pl.ds(j * 128, 128)
                    value = jnp.where(label == cd_ref[:, lanes], ints[rows, lanes], 0.0)
                    hi, lo = halves(value)
                    at = pl.ds(pl.multiple_of(s * 16, 16), 16)
                    parts[q, at, lanes] = hi
                    parts[q, pl.ds(pl.multiple_of(CHUNK + s * 16, 16), 16), lanes] = lo
                return carry

            lax.fori_loop(0, CHUNK // 16, step, 0)

    prepare(0, 3)
    pl.semaphore_wait(barrier, XS * COLS)

    def give(t, carry):
        peer = (place_of + t) % (XS * COLS)
        to_x, to_c = peer // COLS, peer % COLS
        remote(amp_ref.at[to_c, to_x], mine.at[place_of], send.at[0], recv.at[0], to_x * 2 + core, to_c).start()
        return carry

    lax.fori_loop(1, XS * COLS, give, 0)
    own = pltpu.make_async_copy(amp_ref.at[c, x], mine.at[place_of], local_sem.at[0])
    own.start()
    prepare(3, 8)
    own.wait()

    some = mine.at[pl.ds(0, XS * COLS - 1)]
    given = remote(some, some, send.at[0], recv.at[0], r, c)
    given.wait_recv()

    slot = lax.broadcasted_iota(jnp.int32, (CAP, HALF), 0).astype(F32)
    my_rank = jnp.where(core == 0, rank_row[:, 0:HALF], rank_row[:, HALF:NIJ])
    my_key = jnp.where(core == 0, key_col[0], key_col[1])
    pick = jnp.where(my_rank == slot, 1.0, 0.0).astype(BF16)
    for t in range(WIDE // 128):
        cd_row = cd_ref[:, pl.ds(pl.multiple_of(x * WIDE + t * 128, 128), 128)].astype(F32)
        amps = jnp.concatenate([mine[:, t * 2 + i, :] for i in range(2)], axis=0)
        hi, lo = halves(jnp.where(my_key == cd_row, amps, 0.0))
        packed[:, t * 128 : (t + 1) * 128] = dot(pick, hi) + dot(pick, lo)

    remote(packed, gathered.at[r], send.at[2], recv.at[2], sibling, c).start()
    for t in (1, 3, 2):
        remote(packed, gathered.at[r], send.at[3], recv.at[3 + t], (x + t) % 4 * 2 + core, c).start()

    def arrived(k, sem):
        remote(gathered.at[k], gathered.at[k], send.at[3], recv.at[sem], r, c).wait_recv()

    def forward(t):
        k = (x + 4 - t) % 4 * 2 + core
        arrived(k, 3 + t)
        remote(gathered.at[k], gathered.at[k], send.at[7], recv.at[10 + t], sibling, c).start()

    def accumulate(t, finish=None):
        chip = (x + 4 - t) % 4
        if t:
            arrived(chip * 2 + 1 - core, 10 + t)
            values = [gathered[chip * 2], gathered[chip * 2 + 1]]
        else:
            arrived(sibling, 2)
            own, other = packed[...], gathered[sibling]
            values = [jnp.where(core == 0, own, other), jnp.where(core == 0, other, own)]
        weights = jnp.concatenate(halves(jnp.concatenate(values, axis=0)), axis=0)
        lanes = pl.ds(pl.multiple_of(chip * WIDE, WIDE), WIDE)
        for dy, dz in ((2, 1), (2, 0), (1, 1), (3, 1), (1, 0), (3, 0), (0, 1), (0, 0)):
            q = (c // 4 + dy) % 4 * 2 + (c % 4 // 2 + dz) % 2
            both = dot(parts[q, :, lanes], weights, NT)
            both = both[0:CHUNK] + both[CHUNK:]
            if t:
                both += sums[q]
            if finish is None:
                sums[q] = both
            else:
                finish(q, both)

    lane = lax.broadcasted_iota(jnp.int32, (SHARE // 2, 128), 1)

    def finish(q, both):
        both = both + pltpu.roll(both, 2 * CAP, 1)
        for s in range(CHUNK // SHARE):
            to = q * 2 + s
            low = both[s * SHARE : s * SHARE + SHARE // 2]
            high = both[s * SHARE + SHARE // 2 : (s + 1) * SHARE]
            shares[to] = jnp.where(lane < 2 * CAP, low, high)

            @pl.when(to != c)
            def _():
                remote(shares.at[to], got.at[c], send.at[8], recv.at[8], r, to).start()

    accumulate(0)
    forward(1)
    forward(3)
    accumulate(1)
    forward(2)
    accumulate(3)
    accumulate(2, finish)
    own = pltpu.make_async_copy(shares.at[c], got.at[c], local_sem.at[3])
    own.start()
    own.wait()
    some = got.at[pl.ds(0, COLS - 1)]
    drain = remote(some, some, send.at[8], recv.at[8], r, c)
    drain.wait_recv()
    total = got[0]
    for k in range(1, COLS):
        total += got[k]

    ab_row = ab_ref[:, pl.ds(pl.multiple_of(c * SHARE, 128), SHARE)].astype(F32)
    hi, lo = halves(total)
    place = lax.broadcasted_iota(jnp.int32, (HALF, 128), 1).astype(F32)
    for g in range(2):
        slots = rank_col[g * HALF : (g + 1) * HALF] + float(g * CAP)
        pieces = []
        for h in range(2):
            pick = jnp.where(slots + float(h * 2 * CAP) == place, 1.0, 0.0).astype(BF16)
            pieces.append(dot(pick, hi, NT) + dot(pick, lo, NT))
        rows = jnp.where(key_col[g] == ab_row, jnp.concatenate(pieces, axis=1), 0.0)
        for i in range(2):
            fin[:, g, :, i, :] = rows[i * HALF // 2 : (i + 1) * HALF // 2].reshape(XS, COLS, 128)

    me = r * COLS + c

    def hand_out(t, carry):
        peer = (me + t) % (ROWS * COLS)
        to_r, to_c = peer // COLS, peer % COLS
        remote(fin.at[to_r // 2, to_r % 2, to_c], out_ref.at[me], send.at[9], recv.at[9], to_r, to_c).start()
        return carry

    lax.fori_loop(1, ROWS * COLS, hand_out, 0)
    own = pltpu.make_async_copy(fin.at[x, core, c], out_ref.at[me], local_sem.at[4])
    own.start()
    own.wait()
    drain.wait_send()
    some = out_ref.at[pl.ds(0, ROWS * COLS - 1)]
    handed = remote(some, some, send.at[9], recv.at[9], r, c)
    handed.wait_recv()
    handed.wait_send()
    given.wait_send()
    remote(packed, packed, send.at[2], recv.at[2], r, c).wait_send()
    three = gathered.at[pl.ds(0, 3)]
    remote(three, three, send.at[3], recv.at[2], r, c).wait_send()
    remote(three, three, send.at[7], recv.at[2], r, c).wait_send()


def packed_round(base, amps, integrals, ij_irrep, ab_irrep, cd_irrep):
    vmem = pl.BlockSpec(memory_space=pltpu.VMEM)
    hbm = pl.BlockSpec(memory_space=pl.ANY)
    out, most = pl.pallas_call(
        kernel,
        out_shape=(
            jax.ShapeDtypeStruct((ROWS * COLS, 2, 128), F32),
            jax.ShapeDtypeStruct((8, 128), jnp.int32),
        ),
        in_specs=[vmem, hbm, hbm, vmem, vmem, vmem],
        out_specs=(vmem, vmem),
        scratch_shapes=[
            pltpu.VMEM((BLOCK, BLOCK), F32),
            pltpu.VMEM((CHUNKS, 2 * CHUNK, BLOCK), BF16),
            pltpu.VMEM((BLOCK, 128), jnp.int32),
            pltpu.VMEM((XS * COLS, 8, 128), F32),
            pltpu.VMEM((CAP, WIDE), F32),
            pltpu.VMEM((ROWS, CAP, WIDE), F32),
            pltpu.VMEM((CHUNKS, CHUNK, 128), F32),
            pltpu.VMEM((COLS, SHARE // 2, 128), F32),
            pltpu.VMEM((COLS, SHARE // 2, 128), F32),
            pltpu.VMEM((XS, 2, COLS, 2, 128), F32),
            pltpu.SemaphoreType.DMA((CHUNKS,)),
            pltpu.SemaphoreType.DMA((6,)),
            pltpu.SemaphoreType.DMA((14,)),
            pltpu.SemaphoreType.DMA((14,)),
        ],
        compiler_params=pltpu.CompilerParams(collective_id=0, has_side_effects=True, vmem_limit_bytes=58 << 20),
        name="packed_round",
    )(base, amps, integrals, ij_irrep, ab_irrep, cd_irrep)
    return out.transpose(1, 0, 2).reshape(2, ROWS * COLS * 128), most


def body(amplitudes, integrals, ij_irrep, ab_irrep, cd_irrep):
    amps = amplitudes.reshape(2, COLS, XS, 4, 128).transpose(1, 2, 3, 0, 4).reshape(COLS, XS, 8, 128)
    rest = (amps, integrals, ij_irrep.reshape(1, -1), ab_irrep.reshape(1, -1), cd_irrep.reshape(1, -1))
    first = jnp.asarray(np.arange(128, dtype=np.int32)[None, :])
    out, most = packed_round(first, *rest)

    def more(state):
        return state[0] < most[0, 0]

    def another(state):
        base, so_far = state
        return base + CAP, so_far + packed_round(first + base, *rest)[0]

    _, out = lax.while_loop(more, another, (jnp.int32(CAP), out))
    return out


def solution(mesh):
    in_specs = (P(("row", "col"), None), P("row", "col"), P(), P("row"), P("col"))
    out_specs = P(("row", "col"), None)
    return jax.shard_map(body, mesh=mesh, in_specs=in_specs, out_specs=out_specs, check_vma=False)
```

time: 52 us -> 48.4 us (0.931)
  Pallas kernels: 48.3 us -> 45.5 us
  local copies, waits for them, and re-layouts: 2.54 us -> 1.86 us
    pallas_call x1, Pallas kernels: 48.3 us -> 45.5 us  [packed_round(): pl.pallas_call(kernel, out_shape=(jax.ShapeDtypeStruct((ROWS * COLS, 2, 1...]
    broadcast_in_dim x1 -> x0, local copies, waits for them, and re-layouts: 0.59 us -> none  [body(): out, most = packed_round(jnp.zeros((1, 128), jnp.int32), *rest)]
where the time goes in v3:
time: 48.4 us; the launch traced here: 48.2 us
  Pallas kernels  45.5 us (94%)
  local copies, waits for them, and re-layouts  1.86 us (4%)
  loops' own time  0.75 us (2%)
    pallas_call x1, Pallas kernels, packed_round(): pl.pallas_call(kernel, out_shape=(jax.ShapeDtypeStruct((ROWS * COLS, 2, 1...  45.5 us
    slice x1, local copies, waits for them, and re-layouts, more(): return state[0] < most[0, 0]  1.18 us

profile of v3, /device:TPU:1, one launch (start us, length us, event | category | flops | bytes accessed | tf_op | source)
XLA Modules:
  0.0 48.2 jit_solution(7118763973896632582)
XLA Ops:
  0.0 0.0 copy-start.4
  0.0 0.0 copy-start.2
  0.0 0.0 copy-start.1
  0.0 0.0 copy-start.3
  0.0 0.0 copy-start
  0.0 45.5 %packed_round.2 = (f32[128,2,128]{2,1,0:T(2,128)S(1)}, s32[8,128]{1,0:T(8,128)}) custom-call(s32[1,128]{1,0:T(1,128)} %constant.6.clone.base_ref, f32[16,4,8,128]{3,2,1,0:T(8,128)} %bitcast.19, f32[2048,2048]{1,0:T(8,128)} %int_ref.1, s32[1,256]{1,0:T(1,128)} %bitcast.26, s32[1,2048]{1,0:T(1,128)} %bitcast.22, s32[1,2048]{1,0:T(1,128)} %bitcast.24), custom_call_target="tpu_custom_call" | custom-call | tf_op jit(solution)/shard_map/packed_round/pallas_call | solution.py:243
  45.6 0.0 copy-done.4
  45.6 0.0 copy-done.2
  45.6 0.0 copy-done.1
  45.6 0.0 copy-done.3
  45.6 0.0 copy-done
  45.6 1.9 %while.11 = (s32[]{:T(128)}, f32[2,16384]{1,0:T(2,128)S(1)}, s32[8,128]{1,0:T(8,128)}, f32[16,4,8,128]{3,2,1,0:T(8,128)S(1)}, f32[2048,2048]{1,0:T(8,128)}, /*in...) while((s32[]{:T(128)}, f32[2,16384]{1,0:T(2,128)S(1)}, ...), condition=%wide.region_1.0_spmd.clone, body=%wide.region_0.0_spmd.sunk.clone.sunk | while | flops 32898 | bytes 394361 | solution.py:286
  45.6 1.2 %slice.4 = s32[1,1]{1,0:T(1,128)} slice(s32[8,128]{1,0:T(8,128)} %get-tuple-element.114), slice={[0:1], [0:1]} | slice | bytes 8 | tf_op jit(solution)/shard_map/while/cond/slice | solution.py:280
  47.5 0.7 %copy.15 = f32[2,16384]{1,0:T(2,128)} copy(f32[2,16384]{1,0:T(2,128)S(1)} %get-tuple-element.58) | data formatting | bytes 262144
Async XLA Ops:
  0.0 45.6 %copy-start.4 = (s32[1,128]{1,0:T(1,128)S(1)}, s32[1,128]{1,0:T(1,128)}, u32[]{:S(2)}) copy-start(s32[1,128]{1,0:T(1,128)} %constant.6.clone..sunk.2) | copy-start | bytes 1540
  0.0 45.6 %copy-start.2 = (s32[2048]{0:T(1024)S(1)}, s32[2048]{0:T(1024)}, u32[]{:S(2)}) copy-start(s32[2048]{0:T(1024)} %param.12) | copy-start | bytes 24580
  0.0 45.6 %copy-start.1 = (s32[2048]{0:T(1024)S(1)}, s32[2048]{0:T(1024)}, u32[]{:S(2)}) copy-start(s32[2048]{0:T(1024)} %param.11) | copy-start | bytes 24580
  0.0 45.6 %copy-start.3 = (s32[256]{0:T(256)S(1)}, s32[256]{0:T(256)}, u32[]{:S(2)}) copy-start(s32[256]{0:T(256)} %param.10) | copy-start | bytes 3076
  0.0 45.6 %copy-start = (f32[2,32768]{1,0:T(2,128)S(1)}, f32[2,32768]{1,0:T(2,128)}, u32[]{:S(2)}) copy-start(f32[2,32768]{1,0:T(2,128)} %param.8) | copy-start | bytes 786436

commit v4 on v3

--- a/solution.py
+++ b/solution.py
@@ -49,17 +49,22 @@
     x, core = r // 2, r % 2
     sibling = x * 2 + 1 - core
 
+    def far_first(cores):
+        near = lambda d: min(d, 4 - d)
+        offsets = [(dx, dy, dz, dc) for dx in range(4) for dy in range(4) for dz in range(4) for dc in cores if dx or dy or dz or dc]
+        return sorted(offsets, key=lambda o: -(near(o[0]) + near(o[1]) + near(o[2])))
+
+    to_xs = [(x + d) % 4 for d in range(4)]
+    to_ys = [(c // 4 + d) % 4 * 4 for d in range(4)]
+    to_zs = [(c % 4 + d) % 4 for d in range(4)]
+    to_cores = [core, 1 - core]
+
     barrier = pltpu.get_barrier_semaphore()
     place_of = x * COLS + c
     pl.semaphore_signal(barrier, inc=1, device_id=(sibling, c), device_id_type=MESH)
 
-    def greet(t, carry):
-        peer = (place_of + t) % (XS * COLS)
-        pl.semaphore_signal(barrier, inc=1, device_id=(peer // COLS * 2 + core, peer % COLS), device_id_type=MESH)
-        return carry
-
-    lax.fori_loop(1, XS * COLS, greet, 0)
-
+    for dx, dy, dz, dc in far_first((0,)):
+        pl.semaphore_signal(barrier, inc=1, device_id=(to_xs[dx] * 2 + core, to_ys[dy] + to_zs[dz]), device_id_type=MESH)
     def fetch(q):
         rows = pl.ds(q * CHUNK, CHUNK)
         return pltpu.make_async_copy(int_ref.at[rows], ints.at[rows], int_sem.at[q])
@@ -79,7 +84,7 @@
     same = (keys == key_row) & (source // HALF == target // HALF)
     rank_row = jnp.sum(jnp.where(same & (source < target), 1.0, 0.0), axis=0, keepdims=True)
     rank_col = jnp.sum(jnp.where(same & (target < source), 1.0, 0.0), axis=1, keepdims=True)
-    most_ref[...] = jnp.broadcast_to(jnp.max(rank_row, axis=1, keepdims=True) + 1.0, (8, 128)).astype(jnp.int32)
+    most_ref[0, 0] = jnp.max(rank_row).astype(jnp.int32) + 1
     base = base_ref[...].astype(F32)
     rank_row = rank_row - base[0:1, 0:1]
     rank_col = rank_col - base[0:1, 0:1]
@@ -109,13 +114,9 @@
     prepare(0, 3)
     pl.semaphore_wait(barrier, XS * COLS)
 
-    def give(t, carry):
-        peer = (place_of + t) % (XS * COLS)
-        to_x, to_c = peer // COLS, peer % COLS
+    for dx, dy, dz, dc in far_first((0,)):
+        to_x, to_c = to_xs[dx], to_ys[dy] + to_zs[dz]
         remote(amp_ref.at[to_c, to_x], mine.at[place_of], send.at[0], recv.at[0], to_x * 2 + core, to_c).start()
-        return carry
-
-    lax.fori_loop(1, XS * COLS, give, 0)
     own = pltpu.make_async_copy(amp_ref.at[c, x], mine.at[place_of], local_sem.at[0])
     own.start()
     prepare(3, 8)
@@ -215,13 +216,9 @@
 
     me = r * COLS + c
 
-    def hand_out(t, carry):
-        peer = (me + t) % (ROWS * COLS)
-        to_r, to_c = peer // COLS, peer % COLS
-        remote(fin.at[to_r // 2, to_r % 2, to_c], out_ref.at[me], send.at[9], recv.at[9], to_r, to_c).start()
-        return carry
-
-    lax.fori_loop(1, ROWS * COLS, hand_out, 0)
+    for dx, dy, dz, dc in far_first((0, 1)):
+        to_x, to_c, to_core = to_xs[dx], to_ys[dy] + to_zs[dz], to_cores[dc]
+        remote(fin.at[to_x, to_core, to_c], out_ref.at[me], send.at[9], recv.at[9], to_x * 2 + to_core, to_c).start()
     own = pltpu.make_async_copy(fin.at[x, core, c], out_ref.at[me], local_sem.at[4])
     own.start()
     own.wait()
@@ -244,10 +241,10 @@
         kernel,
         out_shape=(
             jax.ShapeDtypeStruct((ROWS * COLS, 2, 128), F32),
-            jax.ShapeDtypeStruct((8, 128), jnp.int32),
+            jax.ShapeDtypeStruct((1, 1), jnp.int32),
         ),
         in_specs=[vmem, hbm, hbm, vmem, vmem, vmem],
-        out_specs=(vmem, vmem),
+        out_specs=(vmem, pl.BlockSpec(memory_space=pltpu.SMEM)),
         scratch_shapes=[
             pltpu.VMEM((BLOCK, BLOCK), F32),
             pltpu.VMEM((CHUNKS, 2 * CHUNK, BLOCK), BF16),

time: 48.4 us -> 44.1 us (0.911)
  Pallas kernels: 45.5 us -> 42.4 us
  local copies, waits for them, and re-layouts: 1.86 us -> 0.68 us
    pallas_call x1, Pallas kernels: 45.5 us -> 42.4 us  [packed_round(): pl.pallas_call(kernel, out_shape=(jax.ShapeDtypeStruct((ROWS * COLS, 2, 1...]
    slice x1 -> x0, local copies, waits for them, and re-layouts: 1.18 us -> none  [more(): return state[0] < most[0, 0]]
where the time goes in v4:
time: 44.1 us; the launch traced here: 44 us
  Pallas kernels  42.4 us (96%)
  loops' own time  0.81 us (2%)
  local copies, waits for them, and re-layouts  0.68 us (2%)
    pallas_call x1, Pallas kernels, packed_round(): pl.pallas_call(kernel, out_shape=(jax.ShapeDtypeStruct((ROWS * COLS, 2, 1...  42.4 us

profile of v4, /device:TPU:1, one launch (start us, length us, event | category | flops | bytes accessed | tf_op | source)
XLA Modules:
  0.0 44.0 jit_solution(11123787105232394450)
XLA Ops:
  0.0 0.0 copy-start.4
  0.0 0.0 copy-start.2
  0.0 0.0 copy-start.1
  0.0 0.0 copy-start.3
  0.0 0.0 copy-start
  0.0 42.4 %packed_round.2 = (f32[128,2,128]{2,1,0:T(2,128)S(1)}, s32[1,1]{1,0:T(1,128)}) custom-call(s32[1,128]{1,0:T(1,128)} %constant.6.clone.base_ref, f32[16,4,8,128]{3,2,1,0:T(8,128)} %bitcast.19, f32[2048,2048]{1,0:T(8,128)} %int_ref.1, s32[1,256]{1,0:T(1,128)} %bitcast.26, s32[1,2048]{1,0:T(1,128)} %bitcast.22, s32[1,2048]{1,0:T(1,128)} %bitcast.24), custom_call_target="tpu_custom_call" | custom-call | tf_op jit(solution)/shard_map/packed_round/pallas_call | solution.py:240
  42.5 0.0 copy-done.4
  42.5 0.0 copy-done.2
  42.5 0.0 copy-done.1
  42.5 0.0 copy-done.3
  42.5 0.0 copy-done
  42.5 0.8 %while.11 = (s32[]{:T(128)}, f32[2,16384]{1,0:T(2,128)S(1)}, s32[1,1]{1,0:T(1,128)}, f32[16,4,8,128]{3,2,1,0:T(8,128)S(1)}, f32[2048,2048]{1,0:T(8,128)}, /*inde...) while((s32[]{:T(128)}, f32[2,16384]{1,0:T(2,128)S(1)}, ...), condition=%wide.region_1.0_spmd.clone, body=%wide.region_0.0_spmd.sunk.clone.sunk | while | flops 32898 | bytes 394353 | solution.py:283
  43.3 0.7 %copy.15 = f32[2,16384]{1,0:T(2,128)} copy(f32[2,16384]{1,0:T(2,128)S(1)} %get-tuple-element.58) | data formatting | bytes 262144
Async XLA Ops:
  0.0 42.5 %copy-start.4 = (s32[1,128]{1,0:T(1,128)S(1)}, s32[1,128]{1,0:T(1,128)}, u32[]{:S(2)}) copy-start(s32[1,128]{1,0:T(1,128)} %constant.6.clone..sunk.2) | copy-start | bytes 1540
  0.0 42.5 %copy-start.2 = (s32[2048]{0:T(1024)S(1)}, s32[2048]{0:T(1024)}, u32[]{:S(2)}) copy-start(s32[2048]{0:T(1024)} %param.12) | copy-start | bytes 24580
  0.0 42.5 %copy-start.1 = (s32[2048]{0:T(1024)S(1)}, s32[2048]{0:T(1024)}, u32[]{:S(2)}) copy-start(s32[2048]{0:T(1024)} %param.11) | copy-start | bytes 24580
  0.0 42.5 %copy-start.3 = (s32[256]{0:T(256)S(1)}, s32[256]{0:T(256)}, u32[]{:S(2)}) copy-start(s32[256]{0:T(256)} %param.10) | copy-start | bytes 3076
  0.0 42.5 %copy-start = (f32[2,32768]{1,0:T(2,128)S(1)}, f32[2,32768]{1,0:T(2,128)}, u32[]{:S(2)}) copy-start(f32[2,32768]{1,0:T(2,128)} %param.8) | copy-start | bytes 786436

commit v5 on v4

--- a/solution.py
+++ b/solution.py
@@ -111,7 +111,7 @@
 
             lax.fori_loop(0, CHUNK // 16, step, 0)
 
-    prepare(0, 3)
+    prepare(0, 2)
     pl.semaphore_wait(barrier, XS * COLS)
 
     for dx, dy, dz, dc in far_first((0,)):
@@ -119,7 +119,7 @@
         remote(amp_ref.at[to_c, to_x], mine.at[place_of], send.at[0], recv.at[0], to_x * 2 + core, to_c).start()
     own = pltpu.make_async_copy(amp_ref.at[c, x], mine.at[place_of], local_sem.at[0])
     own.start()
-    prepare(3, 8)
+    prepare(2, 8)
     own.wait()
 
     some = mine.at[pl.ds(0, XS * COLS - 1)]
@@ -136,9 +136,9 @@
         hi, lo = halves(jnp.where(my_key == cd_row, amps, 0.0))
         packed[:, t * 128 : (t + 1) * 128] = dot(pick, hi) + dot(pick, lo)
 
-    remote(packed, gathered.at[r], send.at[2], recv.at[2], sibling, c).start()
     for t in (1, 3, 2):
         remote(packed, gathered.at[r], send.at[3], recv.at[3 + t], (x + t) % 4 * 2 + core, c).start()
+    remote(packed, gathered.at[r], send.at[2], recv.at[2], sibling, c).start()
 
     def arrived(k, sem):
         remote(gathered.at[k], gathered.at[k], send.at[3], recv.at[sem], r, c).wait_recv()
@@ -159,7 +159,7 @@
             values = [jnp.where(core == 0, own, other), jnp.where(core == 0, other, own)]
         weights = jnp.concatenate(halves(jnp.concatenate(values, axis=0)), axis=0)
         lanes = pl.ds(pl.multiple_of(chip * WIDE, WIDE), WIDE)
-        for dy, dz in ((2, 1), (2, 0), (1, 1), (3, 1), (1, 0), (3, 0), (0, 1), (0, 0)):
+        for dy, dz in ((1,1),(3,0),(2,1),(0,1),(1,0),(3,1),(2,0),(0,0)):
             q = (c // 4 + dy) % 4 * 2 + (c % 4 // 2 + dz) % 2
             both = dot(parts[q, :, lanes], weights, NT)
             both = both[0:CHUNK] + both[CHUNK:]

time: 44.1 us -> 43 us (0.975)
  Pallas kernels: 42.4 us -> 41.3 us
    pallas_call x1, Pallas kernels: 42.4 us -> 41.3 us  [packed_round(): pl.pallas_call(kernel, out_shape=(jax.ShapeDtypeStruct((ROWS * COLS, 2, 1...]
where the time goes in v5:
time: 43 us; the launch traced here: 42.9 us
  Pallas kernels  41.3 us (96%)
  loops' own time  0.81 us (2%)
  local copies, waits for them, and re-layouts  0.68 us (2%)
    pallas_call x1, Pallas kernels, packed_round(): pl.pallas_call(kernel, out_shape=(jax.ShapeDtypeStruct((ROWS * COLS, 2, 1...  41.3 us

profile of v5, /device:TPU:1, one launch (start us, length us, event | category | flops | bytes accessed | tf_op | source)
XLA Modules:
  0.0 42.9 jit_solution(5040871413022259152)
XLA Ops:
  0.0 0.0 copy-start.4
  0.0 0.0 copy-start.2
  0.0 0.0 copy-start.1
  0.0 0.0 copy-start.3
  0.0 0.0 copy-start
  0.0 41.3 %packed_round.2 = (f32[128,2,128]{2,1,0:T(2,128)S(1)}, s32[1,1]{1,0:T(1,128)}) custom-call(s32[1,128]{1,0:T(1,128)} %constant.6.clone.base_ref, f32[16,4,8,128]{3,2,1,0:T(8,128)} %bitcast.19, f32[2048,2048]{1,0:T(8,128)} %int_ref.1, s32[1,256]{1,0:T(1,128)} %bitcast.26, s32[1,2048]{1,0:T(1,128)} %bitcast.22, s32[1,2048]{1,0:T(1,128)} %bitcast.24), custom_call_target="tpu_custom_call" | custom-call | tf_op jit(solution)/shard_map/packed_round/pallas_call | solution.py:240
  41.4 0.0 copy-done.4
  41.4 0.0 copy-done.2
  41.4 0.0 copy-done.1
  41.4 0.0 copy-done.3
  41.4 0.0 copy-done
  41.4 0.8 %while.11 = (s32[]{:T(128)}, f32[2,16384]{1,0:T(2,128)S(1)}, s32[1,1]{1,0:T(1,128)}, f32[16,4,8,128]{3,2,1,0:T(8,128)S(1)}, f32[2048,2048]{1,0:T(8,128)}, /*inde...) while((s32[]{:T(128)}, f32[2,16384]{1,0:T(2,128)S(1)}, ...), condition=%wide.region_1.0_spmd.clone, body=%wide.region_0.0_spmd.sunk.clone.sunk | while | flops 32898 | bytes 394353 | solution.py:283
  42.2 0.7 %copy.15 = f32[2,16384]{1,0:T(2,128)} copy(f32[2,16384]{1,0:T(2,128)S(1)} %get-tuple-element.58) | data formatting | bytes 262144
Async XLA Ops:
  0.0 41.4 %copy-start.4 = (s32[1,128]{1,0:T(1,128)S(1)}, s32[1,128]{1,0:T(1,128)}, u32[]{:S(2)}) copy-start(s32[1,128]{1,0:T(1,128)} %constant.6.clone..sunk.2) | copy-start | bytes 1540
  0.0 41.4 %copy-start.2 = (s32[2048]{0:T(1024)S(1)}, s32[2048]{0:T(1024)}, u32[]{:S(2)}) copy-start(s32[2048]{0:T(1024)} %param.12) | copy-start | bytes 24580
  0.0 41.4 %copy-start.1 = (s32[2048]{0:T(1024)S(1)}, s32[2048]{0:T(1024)}, u32[]{:S(2)}) copy-start(s32[2048]{0:T(1024)} %param.11) | copy-start | bytes 24580
  0.0 41.4 %copy-start.3 = (s32[256]{0:T(256)S(1)}, s32[256]{0:T(256)}, u32[]{:S(2)}) copy-start(s32[256]{0:T(256)} %param.10) | copy-start | bytes 3076
  0.0 41.4 %copy-start = (f32[2,32768]{1,0:T(2,128)S(1)}, f32[2,32768]{1,0:T(2,128)}, u32[]{:S(2)}) copy-start(f32[2,32768]{1,0:T(2,128)} %param.8) | copy-start | bytes 786436

commit v6 on v5

--- a/solution.py
+++ b/solution.py
@@ -119,7 +119,7 @@
         remote(amp_ref.at[to_c, to_x], mine.at[place_of], send.at[0], recv.at[0], to_x * 2 + core, to_c).start()
     own = pltpu.make_async_copy(amp_ref.at[c, x], mine.at[place_of], local_sem.at[0])
     own.start()
-    prepare(2, 8)
+    prepare(2, 7)
     own.wait()
 
     some = mine.at[pl.ds(0, XS * COLS - 1)]
@@ -184,6 +184,7 @@
             def _():
                 remote(shares.at[to], got.at[c], send.at[8], recv.at[8], r, to).start()
 
+    prepare(7, 8)
     accumulate(0)
     forward(1)
     forward(3)

time: 43 us -> 43 us (level)
  no operation moved by 1% of the time
where the time goes in v6:
time: 43 us; the launch traced here: 42.9 us
  Pallas kernels  41.3 us (96%)
  loops' own time  0.81 us (2%)
  local copies, waits for them, and re-layouts  0.68 us (2%)
    pallas_call x1, Pallas kernels, packed_round(): pl.pallas_call(kernel, out_shape=(jax.ShapeDtypeStruct((ROWS * COLS, 2, 1...  41.3 us

profile of v6, /device:TPU:1, one launch (start us, length us, event | category | flops | bytes accessed | tf_op | source)
XLA Modules:
  0.0 42.9 jit_solution(18151524625932510507)
XLA Ops:
  0.0 0.0 copy-start.4
  0.0 0.0 copy-start.2
  0.0 0.0 copy-start.1
  0.0 0.0 copy-start.3
  0.0 0.0 copy-start
  0.0 41.3 %packed_round.2 = (f32[128,2,128]{2,1,0:T(2,128)S(1)}, s32[1,1]{1,0:T(1,128)}) custom-call(s32[1,128]{1,0:T(1,128)} %constant.6.clone.base_ref, f32[16,4,8,128]{3,2,1,0:T(8,128)} %bitcast.19, f32[2048,2048]{1,0:T(8,128)} %int_ref.1, s32[1,256]{1,0:T(1,128)} %bitcast.26, s32[1,2048]{1,0:T(1,128)} %bitcast.22, s32[1,2048]{1,0:T(1,128)} %bitcast.24), custom_call_target="tpu_custom_call" | custom-call | tf_op jit(solution)/shard_map/packed_round/pallas_call | solution.py:241
  41.4 0.0 copy-done.4
  41.4 0.0 copy-done.2
  41.4 0.0 copy-done.1
  41.4 0.0 copy-done.3
  41.4 0.0 copy-done
  41.4 0.8 %while.11 = (s32[]{:T(128)}, f32[2,16384]{1,0:T(2,128)S(1)}, s32[1,1]{1,0:T(1,128)}, f32[16,4,8,128]{3,2,1,0:T(8,128)S(1)}, f32[2048,2048]{1,0:T(8,128)}, /*inde...) while((s32[]{:T(128)}, f32[2,16384]{1,0:T(2,128)S(1)}, ...), condition=%wide.region_1.0_spmd.clone, body=%wide.region_0.0_spmd.sunk.clone.sunk | while | flops 32898 | bytes 394353 | solution.py:284
  42.2 0.7 %copy.15 = f32[2,16384]{1,0:T(2,128)} copy(f32[2,16384]{1,0:T(2,128)S(1)} %get-tuple-element.58) | data formatting | bytes 262144
Async XLA Ops:
  0.0 41.4 %copy-start.4 = (s32[1,128]{1,0:T(1,128)S(1)}, s32[1,128]{1,0:T(1,128)}, u32[]{:S(2)}) copy-start(s32[1,128]{1,0:T(1,128)} %constant.6.clone..sunk.2) | copy-start | bytes 1540
  0.0 41.4 %copy-start.2 = (s32[2048]{0:T(1024)S(1)}, s32[2048]{0:T(1024)}, u32[]{:S(2)}) copy-start(s32[2048]{0:T(1024)} %param.12) | copy-start | bytes 24580
  0.0 41.4 %copy-start.1 = (s32[2048]{0:T(1024)S(1)}, s32[2048]{0:T(1024)}, u32[]{:S(2)}) copy-start(s32[2048]{0:T(1024)} %param.11) | copy-start | bytes 24580
  0.0 41.4 %copy-start.3 = (s32[256]{0:T(256)S(1)}, s32[256]{0:T(256)}, u32[]{:S(2)}) copy-start(s32[256]{0:T(256)} %param.10) | copy-start | bytes 3076
  0.0 41.4 %copy-start = (f32[2,32768]{1,0:T(2,128)S(1)}, f32[2,32768]{1,0:T(2,128)}, u32[]{:S(2)}) copy-start(f32[2,32768]{1,0:T(2,128)} %param.8) | copy-start | bytes 786436
